TPU v7x, 128 devices: a whole 4x4x4 slice. The times are simulated.
128 devices in a mesh: slab: 16 (over x, z), sta: 8 (over y, core).
Axes of the slice: x: 4, y: 4, z: 4, core: 2. Of those that a mesh axis runs over, the one named last changes fastest.
Arguments:
- model_change: float32 [4, 192, 256, 256], P(None, 'slab', 'sta'), may hold values from -6 to 6
- sens_blocks: bfloat16 [16, 8, 640, 128, 128], P('slab', 'sta'), may hold values from -0.01953125 to 0.01953125
- block_rows: int32 [16, 8, 640], P('slab', 'sta'), may hold values from 0 to 127
- block_cols: int32 [16, 8, 640], P('slab', 'sta'), may hold values from 0 to 12287, as said below
- live_count: int32 [16, 8], P('slab', 'sta'), may hold values from 320 to 640, as said below
- owner_order: int32 [128], replicated, may hold values from 0 to 127, each once
Outputs:
- gravity_data: float32 [4, 16384], P(None, ('slab', 'sta'))
Inputs may be any that keep to these rules, and one draw needn't show every extreme that they name: `block_cols`: among one device's 640 entries at most 80 name blocks p * 768 + b of one p, and on every device exactly 80 do for some p. `live_count`: some device has all 640 entries live.
All inputs are finite; a program needn't handle non-finite values.
Results may differ from a plain program's by a relative error of at most 0.0029.
Values may be sent and summed in bfloat16 or wider, within the bound.
A program may use at most 128 MiB of HBM per device.

v0:
```python
import math

import jax
import jax.numpy as jnp
from jax import lax
from jax.sharding import PartitionSpec as P

BLK = 128


FILTER_TAPS = (
    (1.0 + math.sqrt(3.0)) / (4.0 * math.sqrt(2.0)),
    (3.0 + math.sqrt(3.0)) / (4.0 * math.sqrt(2.0)),
    (3.0 - math.sqrt(3.0)) / (4.0 * math.sqrt(2.0)),
    (1.0 - math.sqrt(3.0)) / (4.0 * math.sqrt(2.0)),
)


def shifted(value, axis, steps):
    count = lax.axis_size(axis)
    pairs = [(source, (source + steps) % count) for source in range(count)]
    return lax.ppermute(value, axis, pairs)


def wavelet_axis(values, along, rim_cells):
    length = values.shape[along]
    even_cells = lax.slice_in_dim(values, 0, length, 2, along)
    odd_cells = lax.slice_in_dim(values, 1, length, 2, along)
    half_len = even_cells.shape[along]
    if rim_cells is None:
        next_even = jnp.roll(even_cells, -1, along)
        next_odd = jnp.roll(odd_cells, -1, along)
    else:
        next_even = jnp.concatenate(
            [
                lax.slice_in_dim(even_cells, 1, half_len, 1, along),
                lax.slice_in_dim(rim_cells, 0, 1, 1, along),
            ],
            along,
        )
        next_odd = jnp.concatenate(
            [
                lax.slice_in_dim(odd_cells, 1, half_len, 1, along),
                lax.slice_in_dim(rim_cells, 1, 2, 1, along),
            ],
            along,
        )
    low_band = (
        FILTER_TAPS[0] * even_cells
        + FILTER_TAPS[1] * odd_cells
        + FILTER_TAPS[2] * next_even
        + FILTER_TAPS[3] * next_odd
    )
    high_band = (
        FILTER_TAPS[3] * even_cells
        - FILTER_TAPS[2] * odd_cells
        + FILTER_TAPS[1] * next_even
        - FILTER_TAPS[0] * next_odd
    )
    return jnp.stack([low_band, high_band], along + 1).reshape(values.shape)


def on_device(model_change, sens_blocks, block_rows, block_cols, live_count, owner_order):
    wave_field = wavelet_axis(model_change, 3, None)
    rim_y = shifted(lax.slice_in_dim(wave_field, 0, 2, 1, 2), "sta", -1)
    wave_field = wavelet_axis(wave_field, 2, rim_y)
    field_shape = wave_field.shape
    flat_field = wave_field.reshape(field_shape[0], field_shape[1], field_shape[2] * field_shape[3])
    turned = lax.all_to_all(flat_field, "slab", split_axis=2, concat_axis=1, tiled=True)
    turned = wavelet_axis(turned, 1, None)
    wave_field = (
        lax.all_to_all(turned.astype(jnp.bfloat16), "slab", split_axis=1, concat_axis=2, tiled=True)
        .astype(turned.dtype)
        .reshape(field_shape)
    )
    block_count = field_shape[1] * field_shape[2] * field_shape[3] // BLK
    coef_blocks = wave_field.astype(jnp.bfloat16).reshape(field_shape[0], block_count, BLK)
    col_list = block_cols.reshape(-1)
    row_list = block_rows.reshape(-1)
    live_now = live_count.reshape(())
    entries = col_list.shape[0]
    blocks = sens_blocks.reshape(entries, BLK, BLK)
    gathered = lax.all_gather(coef_blocks, "slab", axis=1, tiled=True)
    picked = jnp.take(gathered, col_list, axis=1)
    block_terms = jnp.einsum("ekc,ksc->kes", picked, blocks, preferred_element_type=jnp.float32)
    keep_mask = jnp.arange(entries, dtype=jnp.int32) < live_now
    route_table = ((owner_order[:, None] == row_list[None, :]) & keep_mask[None, :]).astype(
        jnp.float32
    )
    partial_data = jnp.einsum(
        "bk,kes->ebs", route_table, block_terms, precision=lax.Precision.HIGHEST
    )
    partial_data = partial_data.reshape(field_shape[0], owner_order.shape[0] * BLK)
    return lax.psum_scatter(partial_data, ("slab", "sta"), scatter_dimension=1, tiled=True)


def solution(mesh):
    placed = (
        P(None, "slab", "sta", None),
        P("slab", "sta", None, None, None),
        P("slab", "sta", None),
        P("slab", "sta", None),
        P("slab", "sta"),
        P(),
    )
    return jax.shard_map(
        on_device, mesh=mesh, in_specs=placed, out_specs=P(None, ("slab", "sta")), check_vma=False
    )
```

profile of v0, /device:TPU:1, one launch (start us, length us, event | category | flops | bytes accessed | tf_op | source)
XLA Modules:
  0.0 1071.1 jit_solution(14636418353078076222)
XLA Ops:
  6.5 27.4 %slice.61 = f32[4,12,32,128]{3,2,1,0:T(8,128)S(1)} slice(f32[4,12,32,256]{3,2,1,0:T(8,128)} %param.6), slice={[0:4:1], [0:12:1], [0:32:1], [0:256:2]} | slice | bytes 1572864 | tf_op jit(solution)/shard_map/slice | solution.py:27
  34.0 26.5 %slice.62 = f32[4,12,32,128]{3,2,1,0:T(8,128)S(1)} slice(f32[4,12,32,256]{3,2,1,0:T(8,128)S(1)} %copy-done), slice={[0:4:1], [0:12:1], [0:32:1], [1:256:2]} | slice | bytes 1572864 | tf_op jit(solution)/shard_map/slice | solution.py:28
  61.0 0.7 add_bitcast_fusion.1
  61.8 6.3 copy.87
  68.2 4.4 copy.90
  72.6 1.4 collective-permute-start
  74.0 38.5 %slice.67 = f32[4,12,16,256]{2,3,1,0:T(8,128)} slice(f32[4,12,32,256]{2,3,1,0:T(8,128)} %bitcast.48), slice={[0:4:1], [0:12:1], [0:32:2], [0:256:1]} | slice | bytes 1572864 | tf_op jit(solution)/shard_map/slice | solution.py:27
  112.5 39.2 %slice.68 = f32[4,12,16,256]{2,3,1,0:T(8,128)} slice(f32[4,12,32,256]{2,3,1,0:T(8,128)} %bitcast.49), slice={[0:4:1], [0:12:1], [1:32:2], [0:256:1]} | slice | bytes 1572864 | tf_op jit(solution)/shard_map/slice | solution.py:28
  151.8 4.3 copy.109
  156.2 4.3 copy.110
  160.8 0.5 add_bitcast_fusion
  161.5 8.6 copy.102
  170.1 32.8 %reshape.83 = f32[16,1,24576]{2,1,0:T(1,128)S(1)} reshape(f32[8192,4,12]{2,1,0:T(4,128)} %bitcast.50) | data formatting | bytes 3145728
  202.9 26.5 %all_to_all.36 = f32[16,1,24576]{2,1,0:T(1,128)S(1)} all-to-all(f32[16,1,24576]{2,1,0:T(1,128)S(1)} %reshape.83), channel_id=1, replica_groups=mesh['slab'=16,'sta'=8] {'slab'}, dimensions={0} | all-to-all | bytes 3145728 | tf_op jit(solution)/shard_map/all_to_all | solution.py:69
  229.4 0.5 broadcast.135
  229.9 4.4 reduce.4
  234.3 29.0 %reshape.84 = f32[8192,4,12]{2,1,0:T(4,128)} reshape(f32[16,24576]{1,0:T(8,128)S(1)} %reduce.4) | data formatting | bytes 3145728
  263.3 10.2 copy.103
  273.6 1.0 copy.96
  275.0 1.0 fusion.10
  276.1 0.6 pad_maximum_fusion.8
  276.9 14.2 %all_to_all.37 = bf16[4,192,512]{2,0,1:T(4,128)(2,1)S(1)} all-to-all(bf16[4,192,512]{2,0,1:T(4,128)(2,1)S(1)} %bitcast.58), channel_id=1, replica_groups=mesh['slab'=16,'sta'=8] {'slab'}, dimensions={1} | all-to-all | bytes 1572864 | tf_op jit(solution)/shard_map/all_to_all | solution.py:72
  291.1 0.4 copy.98
  291.5 0.5 all_to_all.33
  292.0 1.5 copy.99
  294.4 94.3 %all-gather.2.cloned.1.call-done = bf16[4,12288,128]{2,0,1:T(4,128)(2,1)} async-done(((bf16[4,768,128]{2,0,1:T(4,128)(2,1)}), bf16[4,12288,128]{2,0,1:T(4,128)(2,1)}) %all-gather.2.cloned.1.call-update) | async-done | bytes 12582928 | tf_op jit(solution)/shard_map/all_gather | solution.py:83
  388.7 6.3 gather_fusion
  395.1 15.3 %fusion = f32[640,4,128]{2,1,0:T(4,128)S(1)} fusion(bf16[1,1,640,128,128]{4,3,2,1,0:T(8,128)(2,1)} %param.7, bf16[640,4,128]{2,1,0:T(4,128)(2,1)S(1)} %gather_fusion, pred[640]{0:T(1024)(128)(4,1)S(1)} %compare_and_fusion), kind=kOutput, calls=%fused_computation.1 | convolution fusion | flops 84213760 | bytes 22938240 | tf_op jit(solution)/shard_map/ekc,ksc->kes/dot_general | solution.py:85
  410.4 1.3 fusion.4
  411.7 7.6 copy.107
  419.3 643.1 %reduce-scatter.4.cloned.1.call-done = f32[128,4]{1,0:T(8,128)} async-done(((f32[16384,4]{1,0:T(8,128)}), f32[128,4]{1,0:T(8,128)}) %reduce-scatter.4.cloned.1.call-update) | async-done | bytes 2064
  1062.4 1.5 copy.105
  (34 shorter events, 1.9 us)
Async XLA Ops:
  6.5 27.5 %copy-start = (f32[4,12,32,256]{3,2,1,0:T(8,128)S(1)}, f32[4,12,32,256]{3,2,1,0:T(8,128)}, u32[]{:S(2)}) copy-start(f32[4,12,32,256]{3,2,1,0:T(8,128)} %param.6) | copy-start | bytes 4718596
  6.5 382.2 %all-gather.2.cloned.1.call-start = ((), (), s32[]{:S(2)}) async-start(), calls=%async_computation.3 | async-start | bytes 13369344 | tf_op jit(solution)/shard_map/all_gather | solution.py:83
  72.6 88.0 %collective-permute-start = (f32[4,12,2,256]{3,0,2,1:T(4,128)S(1)}, f32[4,12,2,256]{3,0,2,1:T(4,128)S(1)}, u32[]{:S(2)}, u32[]{:S(2)}) collective-permute-start(f32[4,12,2,256]{3,0,2,1:T(4,128)S(1)} %copy.90), channel_id=1, source_target_pairs={{0,7},{1,0},{2,1},{3,2},{4,3},{5,4},{6,5},{7,6},{8,15},{9,8},{10,9... | collective-permute-start | bytes 294920 | tf_op jit(solution)/shard_map/ppermute | solution.py:22
  292.0 1.6 copy-start.1
  292.0 1.6 copy-start.2
  293.6 768.8 %reduce-scatter.4.cloned.1.call-start = ((), (), s32[]{:S(2)}) async-start(), calls=%async_computation.4 | async-start | bytes 8454144
  395.0 15.3 %copy-start.3 = (s32[128]{0:T(128)S(1)}, s32[128]{0:T(128)}, u32[]{:S(2)}) copy-start(s32[128]{0:T(128)} %param.11) | copy-start | bytes 1540
Sparse Core Ops, SparseCore 0:
  293.7 94.9 all-gather.1
  419.4 642.8 reduce-scatter.3
where the time goes:
time: 1080 us; the launch traced here: 1070 us
  waiting for transfers between devices  737 us (68%)
  local copies, waits for them, and re-layouts  253 us (23%)
  blocking collectives  40.7 us (4%)
  matrix products  16.6 us (2%)
  between operations  14.8 us (1%)
    unnamed x3, waiting for transfers between devices  643 us
    all_gather x1, waiting for transfers between devices, on_device(): gathered = lax.all_gather(coef_blocks, 'slab', axis=1, tiled=True)  94.3 us
    unnamed x14, local copies, waits for them, and re-layouts  79.7 us
    slice x3, local copies, waits for them, and re-layouts, wavelet_axis(): even_cells = lax.slice_in_dim(values, 0, length, 2, along)  66.2 us
    slice x2, local copies, waits for them, and re-layouts, wavelet_axis(): odd_cells = lax.slice_in_dim(values, 1, length, 2, along)  65.7 us
    all_to_all x1, blocking collectives, on_device(): lax.all_to_all(flat_field, 'slab', split_axis=2, concat_axis=1, tiled=True)  26.5 us
  transfers between devices with their start and end apart: 3, of which 2 were waited for; matrix products, arithmetic and copies ran while one was open for 8% of the time, Pallas kernels for 0%

commit v1 on v0

v1 whole, which is shorter than its diff:
```python
import functools
import math

import jax
import jax.numpy as jnp
import ml_dtypes
import numpy as np
from jax import lax
from jax.experimental import pallas as pl
from jax.experimental.pallas import tpu as pltpu
from jax.sharding import PartitionSpec as P

MESH = pl.DeviceIdType.MESH
F32, BF16, I32 = jnp.float32, jnp.bfloat16, jnp.int32
NT = (((1,), (1,)), ((), ()))
R3 = math.sqrt(3.0)
H0, H1, H2, H3 = (
    (1.0 + R3) / (4.0 * math.sqrt(2.0)),
    (3.0 + R3) / (4.0 * math.sqrt(2.0)),
    (3.0 - R3) / (4.0 * math.sqrt(2.0)),
    (1.0 - R3) / (4.0 * math.sqrt(2.0)),
)
C1, C2 = H3 / H0, H1 / H2

EP, SX, SY, NZ, BLK = 4, 12, 32, 256, 128
K, CAP, CB = 640, 80, 768
NSLAB, NSTA = 16, 8
MSG = CAP * EP
KT = K // BLK


def torus(step):
    dx, dz = divmod(step, 4)
    return min(dx, 4 - dx) + min(dz, 4 - dz)


STEPS = [(0, 0)] + [divmod(s, 4) for s in sorted(range(1, 16), key=lambda s: -torus(s))]


def z_matrix():
    w = np.zeros((NZ, NZ), np.float64)
    for k in range(NZ // 2):
        src = [(2 * k + d) % NZ for d in range(4)]
        for at, lo, hi in zip(src, (H0, H1, H2, H3), (H3, -H2, H1, -H0)):
            w[at, 2 * k] = lo
            w[at, 2 * k + 1] = hi
    top = w.astype(ml_dtypes.bfloat16)
    rest = (w - top.astype(np.float64)).astype(ml_dtypes.bfloat16)
    return np.concatenate([top, top, rest], 0)


def behind_of(i, n):
    dx, dz = STEPS[n]
    return lax.rem(i // 4 + 4 - dx, 4) * 4 + lax.rem(lax.rem(i, 4) + 4 - dz, 4)


def list_kernel(cols, rows, live, owner, req, lists, R):
    i = lax.axis_index("slab")
    behind = functools.partial(behind_of, i)
    sub16 = lax.broadcasted_iota(I32, (16, BLK), 0)
    sub128 = lax.broadcasted_iota(I32, (BLK, BLK), 0)
    lane128 = lax.broadcasted_iota(I32, (BLK, BLK), 1)
    sub8 = lax.broadcasted_iota(I32, (8, BLK), 0)
    lane8 = lax.broadcasted_iota(I32, (8, BLK), 1)
    one = lambda m: jnp.where(m, 1.0, 0.0).astype(BF16)
    peer = jnp.zeros((16, BLK), I32)
    for n in range(NSLAB):
        peer = jnp.where(sub16 == n, behind(n), peer)
    first = peer * CB
    upper = one(sub128 < lane128)
    ties, ranks, rels = [], [], []
    carry = jnp.zeros((16, 1), F32)
    for t in range(KT):
        rel = cols[:, t * BLK : (t + 1) * BLK] - first
        tie = (rel >= 0) & (rel < CB)
        tie_f = jnp.where(tie, 1.0, 0.0)
        ranks.append(jnp.dot(tie_f.astype(BF16), upper, preferred_element_type=F32) + carry)
        carry = carry + jnp.sum(tie_f, axis=1, keepdims=True)
        ties.append(tie_f)
        rels.append(jnp.where(tie, rel, 0))
    count = jnp.broadcast_to(carry, (16, BLK))
    scan = count
    for s in (1, 2, 4, 8):
        scan = scan + jnp.where(sub16 >= s, pltpu.roll(scan, s, 0), 0.0)
    base = scan - count

    place = one(sub128 == owner[...])
    inverse = lax.dot_general(
        lane8.astype(F32).astype(BF16), place, NT, preferred_element_type=F32
    ).astype(BF16)
    live_now = live[0, 0]
    ask = jnp.zeros((32, BLK), F32)
    vals, spots = [], []
    for t in range(KT):
        rank_k = jnp.sum(ties[t] * ranks[t], axis=0, keepdims=True).astype(I32)
        slot_k = jnp.sum(ties[t] * (ranks[t] + sub16.astype(F32) * CAP), axis=0, keepdims=True).astype(I32)
        spots.append(jnp.sum(ties[t] * (ranks[t] + base), axis=0, keepdims=True).astype(I32))
        rel = rels[t]
        cell = (rel & -64) + ((rel & 1) << 5) + ((rel >> 1) & 31)
        pair = jnp.concatenate([(cell >> 3).astype(F32), (cell & 7).astype(F32)], 0).astype(BF16)
        ask = ask + lax.dot_general(pair, one(sub128 == rank_k), NT, preferred_element_type=F32)
        dest = jnp.dot(
            inverse, one(sub128 == rows[:, t * BLK : (t + 1) * BLK]), preferred_element_type=F32
        )
        here = lane8 + t * BLK
        dest = jnp.where(here < live_now, dest, 128.0)
        slot8 = jnp.broadcast_to(slot_k, (8, BLK))
        val = jnp.where(sub8 == 0, here >> 3, here & 7)
        val = jnp.where(sub8 == 2, slot8 >> 3, val)
        val = jnp.where(sub8 == 3, slot8 & 7, val).astype(F32)
        vals.append(jnp.where(sub8 == 4, dest, val).astype(BF16))
    ask = (ask[:16] * 8.0 + ask[16:]).astype(I32)
    for n in range(NSLAB):
        req[n] = ask[n : n + 1]

    for u in range(KT):
        got = jnp.zeros((8, BLK), F32)
        for t in range(KT):
            got = got + lax.dot_general(
                vals[t], one(sub128 + u * BLK == spots[t]), NT, preferred_element_type=F32
            )
        dest = got[4:5].astype(I32)
        R[:, u * BLK : (u + 1) * BLK] = one(sub128 == dest)
        lists[0:1, u * BLK : (u + 1) * BLK] = (got[0:1] * 8.0 + got[1:2]).astype(I32)
        lists[1:2, u * BLK : (u + 1) * BLK] = (got[2:3] * 8.0 + got[3:4]).astype(I32)


def kernel(
    model, sens, req, lists, route_in, wz, out,
    X, sv, wv, Sx, Sy, Sc, Rx, Ry, Rc, D, C, st, send, recv, work, gat, T, R,
    reqin, reqs, lists_s, red, redin, acc, accin,
    lsem, hss, hrs, qss, qrs, ass_, ars, rss, rrs, tss, trs,
):
    i, j = lax.axis_index("slab"), lax.axis_index("sta")
    xx, zz = i // 4, lax.rem(i, 4)

    loads = [
        pltpu.make_async_copy(src, dst, lsem.at[n])
        for n, (src, dst) in enumerate(
            ((model, X), (req.at[0], reqin.at[0]), (wz, wv), (lists, lists_s), (route_in, R), (sens, sv))
        )
    ]
    for cp in loads:
        cp.start()

    def ahead(n):
        dx, dz = STEPS[n]
        return lax.rem(xx + dx, 4) * 4 + lax.rem(zz + dz, 4)

    behind = functools.partial(behind_of, i)

    up_i, down_i = lax.rem(i + 1, NSLAB), lax.rem(i + NSLAB - 1, NSLAB)
    up_j, down_j = lax.rem(j + 1, NSTA), lax.rem(j + NSTA - 1, NSTA)

    bar = pltpu.get_barrier_semaphore()
    for n in range(1, NSLAB):
        pl.semaphore_signal(bar, inc=1, device_id=(ahead(n), j), device_id_type=MESH)
    for t in range(1, NSTA):
        pl.semaphore_signal(bar, inc=1, device_id=(i, lax.rem(j + t, NSTA)), device_id_type=MESH)
    pl.semaphore_signal(bar, inc=1, device_id=(up_i, up_j), device_id_type=MESH)

    loads[0].wait()
    for e in range(EP):
        Sx[e] = H2 * X[e, 0] + H3 * X[e, 1]
    for e in range(EP):
        for x in range(SX):
            Sy[4 * x + e : 4 * x + e + 1, :] = H2 * X[e, x, 0:1, :] + H3 * X[e, x, 1:2, :]
    Sc[0:4, :] = H2 * Sy[0:4, :] + H3 * Sy[4:8, :]
    Sc[4:8, :] = jnp.zeros((4, NZ), F32)

    pl.semaphore_wait(bar, NSLAB - 1 + NSTA - 1 + 1)
    halos = [
        pltpu.make_async_remote_copy(src, dst, hss.at[n], hrs.at[n], device_id=dev, device_id_type=MESH)
        for n, (src, dst, dev) in enumerate(
            ((Sy, Ry, (i, down_j)), (Sc, Rc, (down_i, down_j)), (Sx, Rx, (down_i, j)))
        )
    ]
    for cp in halos:
        cp.start()
    asks = [
        pltpu.make_async_remote_copy(
            req.at[n], reqin.at[n], qss.at[n], qrs.at[n], device_id=(behind(n), j), device_id_type=MESH
        )
        for n in range(1, NSLAB)
    ]
    for cp in asks:
        cp.start()

    def spread(x, e, q, val):
        for z in range(2):
            D[z, x, pl.ds(32 * q + e, 8, stride=4), :] = val[:, z * BLK : (z + 1) * BLK]

    def x_pair(k, _):
        for e in range(EP):
            for q in range(SY // 8):
                at = slice(8 * q, 8 * q + 8)
                s = H0 * X[e, 2 * k, at, :] + H1 * X[e, 2 * k + 1, at, :]
                t = H2 * X[e, 2 * k + 2, at, :] + H3 * X[e, 2 * k + 3, at, :]
                spread(2 * k, e, q, s + t)
                spread(2 * k + 1, e, q, C1 * s + C2 * t)
        return 0

    lax.fori_loop(0, SX // 2 - 1, x_pair, 0)

    halos[0].wait_recv()
    halos[1].wait_recv()
    for k in range(SX // 2):
        s = H0 * Ry[8 * k : 8 * k + 4, :] + H1 * Ry[8 * k + 4 : 8 * k + 8, :]
        if k < SX // 2 - 1:
            t = H2 * Ry[8 * k + 8 : 8 * k + 12, :] + H3 * Ry[8 * k + 12 : 8 * k + 16, :]
        else:
            t = Rc[0:4, :]
        lo, hi = s + t, C1 * s + C2 * t
        for z in range(2):
            at = slice(z * BLK, (z + 1) * BLK)
            D[z, 2 * k, SY * 4 : SY * 4 + 4, :] = lo[:, at]
            D[z, 2 * k + 1, SY * 4 : SY * 4 + 4, :] = hi[:, at]

    low = lax.broadcasted_iota(I32, (8, BLK), 0) < 4
    ca, cb = jnp.where(low, H0, -H2), jnp.where(low, H1, H3)
    cc, cd = jnp.where(low, H2, -H0), jnp.where(low, H3, H1)
    ce = jnp.where(low, 1.0, C2)
    loads[2].wait()

    def yz(x, _):
        parts = []
        for z in range(2):
            v = D[z, x, 0 : SY * 4, :].reshape(SY // 2, 8, BLK)
            u = pltpu.roll(v, 4, 1)
            s = ca * v + cb * u
            t = cc * v[1:] + cd * u[1:]
            rim = D[z, x, SY * 4 : SY * 4 + 4, :]
            last = ce * jnp.concatenate([rim, rim], 0)
            parts.append((s + jnp.concatenate([t, last[None]], 0)).reshape(SY * 4, BLK))
        full = jnp.concatenate(parts, 1)
        high = full.astype(BF16)
        rest = (full - high.astype(F32)).astype(BF16)
        res = jnp.dot(jnp.concatenate([high, rest, high], 1), wv[...], preferred_element_type=F32)
        at = pl.multiple_of(x * 2 * SY * 4, 2 * SY * 4)
        C[pl.ds(at, SY * 4), :] = res[:, :BLK]
        C[pl.ds(at + SY * 4, SY * 4), :] = res[:, BLK:]
        return 0

    lax.fori_loop(0, SX - 2, yz, 0)
    halos[2].wait_recv()
    for e in range(EP):
        for q in range(SY // 8):
            at = slice(8 * q, 8 * q + 8)
            s = H0 * X[e, SX - 2, at, :] + H1 * X[e, SX - 1, at, :]
            t = Rx[e, at, :]
            spread(SX - 2, e, q, s + t)
            spread(SX - 1, e, q, C1 * s + C2 * t)
    lax.fori_loop(SX - 2, SX, yz, 0)

    loads[1].wait()
    for cp in asks:
        cp.wait_recv()
    to_r = pltpu.make_async_copy(reqin, reqs, lsem.at[8])
    to_r.start()
    to_r.wait()
    loads[3].wait()

    def pack(n):
        def some(g, _):
            for a in range(8):
                c = reqs[n, 0, g * 8 + a]
                st[g, 4 * a : 4 * a + 4, :] = C[pl.ds(c * 4, 4), :]
            return 0

        lax.fori_loop(0, CAP // 8, some, 0)

    msgs = []
    for n in list(range(1, NSLAB)) + [0]:
        pack(n)
        if n == 0:
            work[0:MSG, :] = st[...].reshape(MSG, BLK).astype(BF16).astype(F32)
            break
        send[n] = st[...].reshape(MSG, BLK).astype(BF16)
        cp = pltpu.make_async_remote_copy(
            send.at[n], recv.at[n], ass_.at[n], ars.at[n], device_id=(ahead(n), j), device_id_type=MESH
        )
        cp.start()
        msgs.append(cp)

    loads[5].wait()
    loads[4].wait()
    first_half = lax.broadcasted_iota(I32, (8, BLK), 0) < 4
    HALF = CAP // 2

    def products(g, _):
        for a in range(HALF):
            c = lists_s[1, g * HALF + a]
            gat[4 * a : 4 * a + 4, :] = work[pl.ds(c * 4, 4), :]
        for a in range(0, HALF, 2):
            lhs = gat[4 * a : 4 * a + 8, :].astype(BF16)
            rhs = jnp.concatenate([sv[lists_s[0, g * HALF + a]], sv[lists_s[0, g * HALF + a + 1]]], 0)
            res = lax.dot_general(lhs, rhs, NT, preferred_element_type=F32)
            at = pl.multiple_of(g * HALF * 4, HALF * 4) + 4 * a
            T[pl.ds(at, 8), :] = jnp.where(first_half, res[:, :BLK], res[:, BLK:])
        return 0

    def route(lo, hi):
        sums = []
        for e in range(EP):
            term = T[pl.ds(lo * 4 + e, hi - lo, stride=4), :]
            high = term.astype(BF16)
            rest = (term - high.astype(F32)).astype(BF16)
            r = R[:, lo:hi]
            sums.append(
                jnp.dot(r, high, preferred_element_type=F32) + jnp.dot(r, rest, preferred_element_type=F32)
            )
        return sums

    for n in range(1, NSLAB):
        msgs[n - 1].wait_recv()
        work[n * MSG : (n + 1) * MSG, :] = recv[n].astype(F32)
        if n >= NSLAB // 2:
            c = n - NSLAB // 2
            lax.fori_loop(2 * c, 2 * c + 2, products, 0)
        if n == NSLAB - 2:
            for e, part in enumerate(route(0, 512)):
                red[pl.ds(e, BLK, stride=4), :] = part
    for e, part in enumerate(route(512, K)):
        red[pl.ds(e, BLK, stride=4), :] = red[pl.ds(e, BLK, stride=4), :] + part

    sums = []
    for n in range(1, NSLAB):
        p = ahead(n)
        cp = pltpu.make_async_remote_copy(
            red.at[pl.ds(pl.multiple_of(p * 32, 32), 32), :], redin.at[n],
            rss.at[n], rrs.at[n], device_id=(p, j), device_id_type=MESH,
        )
        cp.start()
        sums.append(cp)
    total = red[pl.ds(pl.multiple_of(i * 32, 32), 32), :]
    for n in range(1, NSLAB):
        sums[n - 1].wait_recv()
        total = total + redin[n]
    for q in range(NSTA):
        acc[q] = total[4 * q : 4 * q + 4]
    lasts = []
    for t in range(1, NSTA):
        q = lax.rem(j + t, NSTA)
        cp = pltpu.make_async_remote_copy(
            acc.at[q], accin.at[t], tss.at[t], trs.at[t], device_id=(i, q), device_id_type=MESH
        )
        cp.start()
        lasts.append(cp)
    final = acc[j]
    for t in range(1, NSTA):
        lasts[t - 1].wait_recv()
        final = final + accin[t]
    out[...] = final
    for cp in halos + asks + msgs + sums + lasts:
        cp.wait_send()


def on_device(model_change, sens_blocks, block_rows, block_cols, live_count, owner_order):
    anyspace = pl.BlockSpec(memory_space=pl.ANY)
    dma = pltpu.SemaphoreType.DMA
    vm = pltpu.VMEM
    req, lists, routes = pl.pallas_call(
        list_kernel,
        out_shape=(
            jax.ShapeDtypeStruct((NSLAB, 1, BLK), I32),
            jax.ShapeDtypeStruct((2, K), I32),
            jax.ShapeDtypeStruct((BLK, K), BF16),
        ),
        in_specs=[
            pl.BlockSpec(memory_space=pltpu.SMEM if n == 2 else pltpu.VMEM) for n in range(4)
        ],
        out_specs=[pl.BlockSpec(memory_space=pltpu.VMEM)] * 3,
        name="lists",
    )(
        block_cols.reshape(1, K),
        block_rows.reshape(1, K),
        live_count.reshape(1, 1),
        owner_order.reshape(1, BLK),
    )
    return pl.pallas_call(
        kernel,
        out_shape=jax.ShapeDtypeStruct((EP, BLK), F32),
        in_specs=[anyspace] * 6,
        out_specs=pl.BlockSpec(memory_space=pltpu.VMEM),
        scratch_shapes=[
            vm((EP, SX, SY, NZ), F32), vm((K, BLK, BLK), BF16), vm((3 * NZ, NZ), BF16),
            vm((EP, SY, NZ), F32), vm((SX * 4, NZ), F32), vm((8, NZ), F32),
            vm((EP, SY, NZ), F32), vm((SX * 4, NZ), F32), vm((8, NZ), F32),
            vm((2, SX, SY * 4 + 8, BLK), F32), vm((CB * 4, BLK), F32),
            vm((CAP // 8, 32, BLK), F32), vm((NSLAB, MSG, BLK), BF16), vm((NSLAB, MSG, BLK), BF16),
            vm((NSLAB * MSG, BLK), F32), vm((MSG // 2, BLK), F32), vm((K * 4, BLK), F32), vm((BLK, K), BF16),
            vm((NSLAB, 1, BLK), I32), pltpu.SMEM((NSLAB, 1, BLK), I32),
            pltpu.SMEM((2, K), I32),
            vm((BLK * 4, BLK), F32), vm((NSLAB, 32, BLK), F32),
            vm((NSTA, 4, BLK), F32), vm((NSTA, 4, BLK), F32),
            dma((9,)), dma((3,)), dma((3,)), dma((NSLAB,)), dma((NSLAB,)), dma((NSLAB,)), dma((NSLAB,)),
            dma((NSLAB,)), dma((NSLAB,)), dma((NSTA,)), dma((NSTA,)),
        ],
        compiler_params=pltpu.CompilerParams(
            collective_id=0, has_side_effects=True, vmem_limit_bytes=52 * 2**20
        ),
        name="gravity_step",
    )(
        model_change,
        sens_blocks.reshape(K, BLK, BLK),
        req,
        lists,
        routes,
        jnp.asarray(z_matrix()),
    )


def solution(mesh):
    placed = (
        P(None, "slab", "sta", None),
        P("slab", "sta", None, None, None),
        P("slab", "sta", None),
        P("slab", "sta", None),
        P("slab", "sta"),
        P(),
    )
    return jax.shard_map(
        on_device, mesh=mesh, in_specs=placed, out_specs=P(None, ("slab", "sta")), check_vma=False
    )
```

time: 1080 us -> 59.1 us (0.05)
  waiting for transfers between devices: 737 us -> 0 us
  local copies, waits for them, and re-layouts: 253 us -> 3.88 us
  Pallas kernels: 0 us -> 54.3 us
  blocking collectives: 40.7 us -> 0 us
  matrix products: 16.6 us -> 0 us
  between operations: 14.8 us -> 0.66 us
    unnamed x3 -> x0, waiting for transfers between devices: 643 us -> none
    slice x17 -> x0, local copies, waits for them, and re-layouts: 137 us -> none  [the longest x3 66.2 us: wavelet_axis(): even_cells = lax.slice_in_dim(values, 0, length, 2, along)]
    all_gather x1 -> x0, waiting for transfers between devices: 94.3 us -> none  [on_device(): gathered = lax.all_gather(coef_blocks, 'slab', axis=1, tiled=True)]
    unnamed x14 -> x9, local copies, waits for them, and re-layouts: 79.7 us -> 3.88 us
    pallas_call x0 -> x2, Pallas kernels: none -> 54.3 us  [the longest x1 52 us: on_device(): pl.pallas_call(kernel, out_shape=jax.ShapeDtypeStruct((EP, BLK), F32), in...]
    all_to_all x2 -> x0, blocking collectives: 40.7 us -> none  [the longest x1 26.5 us: on_device(): lax.all_to_all(flat_field, 'slab', split_axis=2, concat_axis=1, tiled=True)]
    dot_general x2 -> x0, matrix products: 16.6 us -> none  [the longest x1 15.3 us: on_device(): jnp.einsum('ekc,ksc->kes', picked, blocks, preferred_element_type=jnp.flo...]
    another operation x3 -> x0, local copies, waits for them, and re-layouts: 15.2 us -> none  [the longest x1 8.57 us: on_device(): wave_field.reshape(field_shape[0], field_shape[1], field_shape[2] * field...]
  transfers between devices with their start and end apart: 3 -> 0, of which waited for: 2 -> 0; matrix products, arithmetic and copies ran while one was open for 8% -> 0% of each run, Pallas kernels for 0% -> 0%
where the time goes in v1:
time: 59.1 us; the launch traced here: 58.9 us
  Pallas kernels  54.3 us (92%)
  local copies, waits for them, and re-layouts  3.88 us (7%)
  between operations  0.66 us (1%)
    pallas_call x1, Pallas kernels, on_device(): pl.pallas_call(kernel, out_shape=jax.ShapeDtypeStruct((EP, BLK), F32), in...  52 us
    unnamed x9, local copies, waits for them, and re-layouts  3.88 us
    pallas_call x1, Pallas kernels, on_device(): pl.pallas_call(list_kernel, out_shape=(jax.ShapeDtypeStruct((NSLAB, 1, BL...  2.32 us

profile of v1, /device:TPU:1, one launch (start us, length us, event | category | flops | bytes accessed | tf_op | source)
XLA Modules:
  0.0 58.9 jit_solution(5864930233460960045)
XLA Ops:
  0.7 2.3 %lists.1 = (s32[16,1,128]{2,1,0:T(1,128)}, s32[2,640]{1,0:T(2,128)}, bf16[128,640]{1,0:T(8,128)(2,1)}) custom-call(s32[1,640]{1,0:T(1,128)} %bitcast.5, s32[1,640]{1,0:T(1,128)} %bitcast.6, s32[1,1]{1,0:T(1,128)S(6)} %copy.9.live, s32[1,128]{1,0:T(1,128)} %bitcast.7), custom_call_target="tpu_custom_call" | custom-call | tf_op jit(solution)/shard_map/lists/pallas_call | solution.py:362
  3.0 0.0 copy-start
  3.0 1.0 %copy-done = bf16[768,256]{1,0:T(8,128)(2,1)S(1)} copy-done((bf16[768,256]{1,0:T(8,128)(2,1)S(1)}, bf16[768,256]{1,0:T(8,128)(2,1)}, u32[]{:S(2)}) %copy-start) | copy-done | bytes 393240
  4.0 0.0 copy-start.1
  4.0 0.9 %copy-done.1 = bf16[128,640]{1,0:T(8,128)(2,1)S(1)} copy-done((bf16[128,640]{1,0:T(8,128)(2,1)S(1)}, bf16[128,640]{1,0:T(8,128)(2,1)}, u32[]{:S(2)}) %copy-start.1) | copy-done | bytes 163864
  4.9 0.0 copy-start.2
  4.9 0.7 %copy-done.2 = s32[16,1,128]{2,1,0:T(1,128)S(1)} copy-done((s32[16,1,128]{2,1,0:T(1,128)S(1)}, s32[16,1,128]{2,1,0:T(1,128)}, u32[]{:S(2)}) %copy-start.2) | copy-done | bytes 8216
  5.6 0.0 copy-start.3
  5.6 0.7 %copy-done.3 = s32[2,640]{1,0:T(2,128)S(1)} copy-done((s32[2,640]{1,0:T(2,128)S(1)}, s32[2,640]{1,0:T(2,128)}, u32[]{:S(2)}) %copy-start.3) | copy-done | bytes 5144
  6.3 52.0 %gravity_step.1 = f32[4,128]{1,0:T(4,128)S(1)} custom-call(f32[4,12,32,256]{3,2,1,0:T(8,128)} %model.1, bf16[640,128,128]{2,1,0:T(8,128)(2,1)} %bitcast.4, s32[16,1,128]{2,1,0:T(1,128)S(1)} %copy-done.2, s32[2,640]{1,0:T(2,128)S(1)} %copy-done.3, bf16[128,640]{1,0:T(8,128)(2,1)S(1)} %copy-done.1, bf16[768,256]{1,0:T(8,128)(2,1)S(1)} %copy-done), custom_call_target="tpu_custom_call" | custom-call | tf_op jit(solution)/shard_map/gravity_step/pallas_call | solution.py:380
  58.3 0.6 copy.10
Async XLA Ops:
  3.0 1.0 %copy-start = (bf16[768,256]{1,0:T(8,128)(2,1)S(1)}, bf16[768,256]{1,0:T(8,128)(2,1)}, u32[]{:S(2)}) copy-start(bf16[768,256]{1,0:T(8,128)(2,1)} %constant.2.clone.wz) | copy-start | bytes 1179652
  4.0 0.9 %copy-start.1 = (bf16[128,640]{1,0:T(8,128)(2,1)S(1)}, bf16[128,640]{1,0:T(8,128)(2,1)}, u32[]{:S(2)}) copy-start(bf16[128,640]{1,0:T(8,128)(2,1)} %get-tuple-element.10.route_in) | copy-start | bytes 491524
  4.9 0.7 %copy-start.2 = (s32[16,1,128]{2,1,0:T(1,128)S(1)}, s32[16,1,128]{2,1,0:T(1,128)}, u32[]{:S(2)}) copy-start(s32[16,1,128]{2,1,0:T(1,128)} %get-tuple-element.8.req) | copy-start | bytes 24580
  5.6 0.7 %copy-start.3 = (s32[2,640]{1,0:T(2,128)S(1)}, s32[2,640]{1,0:T(2,128)}, u32[]{:S(2)}) copy-start(s32[2,640]{1,0:T(2,128)} %get-tuple-element.9.lists) | copy-start | bytes 15364

commit v2 on v1

--- a/solution.py
+++ b/solution.py
@@ -49,14 +49,44 @@
     return np.concatenate([top, top, rest], 0)
 
 
-def behind_of(i, n):
-    dx, dz = STEPS[n]
-    return lax.rem(i // 4 + 4 - dx, 4) * 4 + lax.rem(lax.rem(i, 4) + 4 - dz, 4)
-
-
-def list_kernel(cols, rows, live, owner, req, lists, R):
-    i = lax.axis_index("slab")
-    behind = functools.partial(behind_of, i)
+def kernel(
+    model, sens, cols, rows, live, owner, wz, out,
+    X, sv, wv, cv, rv, ov, lv, Sx, Sy, Sc, Rx, Ry, Rc, D, C, st, send, recv, work, gat, T, R,
+    reqv, reqin, reqs, lists, lists_s, red, redin, acc, accin,
+    lsem, hss, hrs, qss, qrs, ass_, ars, rss, rrs, tss, trs,
+):
+    i, j = lax.axis_index("slab"), lax.axis_index("sta")
+    xx, zz = i // 4, lax.rem(i, 4)
+
+    loads = [
+        pltpu.make_async_copy(src, dst, lsem.at[n])
+        for n, (src, dst) in enumerate(
+            ((cols, cv), (rows, rv), (owner, ov), (live, lv), (model, X), (wz, wv), (sens, sv))
+        )
+    ]
+    for cp in loads:
+        cp.start()
+
+    def ahead(n):
+        dx, dz = STEPS[n]
+        return lax.rem(xx + dx, 4) * 4 + lax.rem(zz + dz, 4)
+
+    def behind(n):
+        dx, dz = STEPS[n]
+        return lax.rem(xx + 4 - dx, 4) * 4 + lax.rem(zz + 4 - dz, 4)
+
+    up_i, down_i = lax.rem(i + 1, NSLAB), lax.rem(i + NSLAB - 1, NSLAB)
+    up_j, down_j = lax.rem(j + 1, NSTA), lax.rem(j + NSTA - 1, NSTA)
+
+    bar = pltpu.get_barrier_semaphore()
+    for n in range(1, NSLAB):
+        pl.semaphore_signal(bar, inc=1, device_id=(ahead(n), j), device_id_type=MESH)
+    for t in range(1, NSTA):
+        pl.semaphore_signal(bar, inc=1, device_id=(i, lax.rem(j + t, NSTA)), device_id_type=MESH)
+    pl.semaphore_signal(bar, inc=1, device_id=(up_i, up_j), device_id_type=MESH)
+
+    for cp in loads[:4]:
+        cp.wait()
     sub16 = lax.broadcasted_iota(I32, (16, BLK), 0)
     sub128 = lax.broadcasted_iota(I32, (BLK, BLK), 0)
     lane128 = lax.broadcasted_iota(I32, (BLK, BLK), 1)
@@ -71,7 +101,7 @@
     ties, ranks, rels = [], [], []
     carry = jnp.zeros((16, 1), F32)
     for t in range(KT):
-        rel = cols[:, t * BLK : (t + 1) * BLK] - first
+        rel = cv[:, t * BLK : (t + 1) * BLK] - first
         tie = (rel >= 0) & (rel < CB)
         tie_f = jnp.where(tie, 1.0, 0.0)
         ranks.append(jnp.dot(tie_f.astype(BF16), upper, preferred_element_type=F32) + carry)
@@ -84,23 +114,23 @@
         scan = scan + jnp.where(sub16 >= s, pltpu.roll(scan, s, 0), 0.0)
     base = scan - count
 
-    place = one(sub128 == owner[...])
+    place = one(sub128 == ov[...])
     inverse = lax.dot_general(
         lane8.astype(F32).astype(BF16), place, NT, preferred_element_type=F32
     ).astype(BF16)
-    live_now = live[0, 0]
+    live_now = lv[0, 0]
     ask = jnp.zeros((32, BLK), F32)
     vals, spots = [], []
     for t in range(KT):
         rank_k = jnp.sum(ties[t] * ranks[t], axis=0, keepdims=True).astype(I32)
-        slot_k = jnp.sum(ties[t] * (ranks[t] + sub16.astype(F32) * CAP), axis=0, keepdims=True).astype(I32)
+        slot_k = jnp.sum(ties[t] * (jnp.minimum(ranks[t], CAP - 1.0) + sub16.astype(F32) * CAP), axis=0, keepdims=True).astype(I32)
         spots.append(jnp.sum(ties[t] * (ranks[t] + base), axis=0, keepdims=True).astype(I32))
         rel = rels[t]
         cell = (rel & -64) + ((rel & 1) << 5) + ((rel >> 1) & 31)
         pair = jnp.concatenate([(cell >> 3).astype(F32), (cell & 7).astype(F32)], 0).astype(BF16)
         ask = ask + lax.dot_general(pair, one(sub128 == rank_k), NT, preferred_element_type=F32)
         dest = jnp.dot(
-            inverse, one(sub128 == rows[:, t * BLK : (t + 1) * BLK]), preferred_element_type=F32
+            inverse, one(sub128 == rv[:, t * BLK : (t + 1) * BLK]), preferred_element_type=F32
         )
         here = lane8 + t * BLK
         dest = jnp.where(here < live_now, dest, 128.0)
@@ -109,57 +139,14 @@
         val = jnp.where(sub8 == 2, slot8 >> 3, val)
         val = jnp.where(sub8 == 3, slot8 & 7, val).astype(F32)
         vals.append(jnp.where(sub8 == 4, dest, val).astype(BF16))
-    ask = (ask[:16] * 8.0 + ask[16:]).astype(I32)
+    ask = jnp.clip((ask[:16] * 8.0 + ask[16:]).astype(I32), 0, CB - 1)
     for n in range(NSLAB):
-        req[n] = ask[n : n + 1]
-
-    for u in range(KT):
-        got = jnp.zeros((8, BLK), F32)
-        for t in range(KT):
-            got = got + lax.dot_general(
-                vals[t], one(sub128 + u * BLK == spots[t]), NT, preferred_element_type=F32
-            )
-        dest = got[4:5].astype(I32)
-        R[:, u * BLK : (u + 1) * BLK] = one(sub128 == dest)
-        lists[0:1, u * BLK : (u + 1) * BLK] = (got[0:1] * 8.0 + got[1:2]).astype(I32)
-        lists[1:2, u * BLK : (u + 1) * BLK] = (got[2:3] * 8.0 + got[3:4]).astype(I32)
-
-
-def kernel(
-    model, sens, req, lists, route_in, wz, out,
-    X, sv, wv, Sx, Sy, Sc, Rx, Ry, Rc, D, C, st, send, recv, work, gat, T, R,
-    reqin, reqs, lists_s, red, redin, acc, accin,
-    lsem, hss, hrs, qss, qrs, ass_, ars, rss, rrs, tss, trs,
-):
-    i, j = lax.axis_index("slab"), lax.axis_index("sta")
-    xx, zz = i // 4, lax.rem(i, 4)
-
-    loads = [
-        pltpu.make_async_copy(src, dst, lsem.at[n])
-        for n, (src, dst) in enumerate(
-            ((model, X), (req.at[0], reqin.at[0]), (wz, wv), (lists, lists_s), (route_in, R), (sens, sv))
-        )
-    ]
-    for cp in loads:
-        cp.start()
-
-    def ahead(n):
-        dx, dz = STEPS[n]
-        return lax.rem(xx + dx, 4) * 4 + lax.rem(zz + dz, 4)
-
-    behind = functools.partial(behind_of, i)
-
-    up_i, down_i = lax.rem(i + 1, NSLAB), lax.rem(i + NSLAB - 1, NSLAB)
-    up_j, down_j = lax.rem(j + 1, NSTA), lax.rem(j + NSTA - 1, NSTA)
-
-    bar = pltpu.get_barrier_semaphore()
-    for n in range(1, NSLAB):
-        pl.semaphore_signal(bar, inc=1, device_id=(ahead(n), j), device_id_type=MESH)
-    for t in range(1, NSTA):
-        pl.semaphore_signal(bar, inc=1, device_id=(i, lax.rem(j + t, NSTA)), device_id_type=MESH)
-    pl.semaphore_signal(bar, inc=1, device_id=(up_i, up_j), device_id_type=MESH)
-
-    loads[0].wait()
+        if n == 0:
+            reqin[n] = ask[n : n + 1]
+        else:
+            reqv[n] = ask[n : n + 1]
+
+    loads[4].wait()
     for e in range(EP):
         Sx[e] = H2 * X[e, 0] + H3 * X[e, 1]
     for e in range(EP):
@@ -179,7 +166,7 @@
         cp.start()
     asks = [
         pltpu.make_async_remote_copy(
-            req.at[n], reqin.at[n], qss.at[n], qrs.at[n], device_id=(behind(n), j), device_id_type=MESH
+            reqv.at[n], reqin.at[n], qss.at[n], qrs.at[n], device_id=(behind(n), j), device_id_type=MESH
         )
         for n in range(1, NSLAB)
     ]
@@ -201,6 +188,24 @@
         return 0
 
     lax.fori_loop(0, SX // 2 - 1, x_pair, 0)
+
+    order = []
+    for u in range(KT):
+        got = jnp.zeros((8, BLK), F32)
+        for t in range(KT):
+            got = got + lax.dot_general(
+                vals[t], one(sub128 + u * BLK == spots[t]), NT, preferred_element_type=F32
+            )
+        dest = got[4:5].astype(I32)
+        R[:, u * BLK : (u + 1) * BLK] = one(sub128 == dest)
+        lists[0:1, u * BLK : (u + 1) * BLK] = jnp.clip(
+            (got[0:1] * 8.0 + got[1:2]).astype(I32), 0, K - 1
+        )
+        lists[1:2, u * BLK : (u + 1) * BLK] = jnp.clip(
+            (got[2:3] * 8.0 + got[3:4]).astype(I32), 0, NSLAB * CAP - 1
+        )
+    to_s = pltpu.make_async_copy(lists, lists_s, lsem.at[7])
+    to_s.start()
 
     halos[0].wait_recv()
     halos[1].wait_recv()
@@ -220,7 +225,7 @@
     ca, cb = jnp.where(low, H0, -H2), jnp.where(low, H1, H3)
     cc, cd = jnp.where(low, H2, -H0), jnp.where(low, H3, H1)
     ce = jnp.where(low, 1.0, C2)
-    loads[2].wait()
+    loads[5].wait()
 
     def yz(x, _):
         parts = []
@@ -252,13 +257,12 @@
             spread(SX - 1, e, q, C1 * s + C2 * t)
     lax.fori_loop(SX - 2, SX, yz, 0)
 
-    loads[1].wait()
     for cp in asks:
         cp.wait_recv()
     to_r = pltpu.make_async_copy(reqin, reqs, lsem.at[8])
     to_r.start()
     to_r.wait()
-    loads[3].wait()
+    to_s.wait()
 
     def pack(n):
         def some(g, _):
@@ -282,8 +286,7 @@
         cp.start()
         msgs.append(cp)
 
-    loads[5].wait()
-    loads[4].wait()
+    loads[6].wait()
     first_half = lax.broadcasted_iota(I32, (8, BLK), 0) < 4
     HALF = CAP // 2
 
@@ -359,38 +362,21 @@
     anyspace = pl.BlockSpec(memory_space=pl.ANY)
     dma = pltpu.SemaphoreType.DMA
     vm = pltpu.VMEM
-    req, lists, routes = pl.pallas_call(
-        list_kernel,
-        out_shape=(
-            jax.ShapeDtypeStruct((NSLAB, 1, BLK), I32),
-            jax.ShapeDtypeStruct((2, K), I32),
-            jax.ShapeDtypeStruct((BLK, K), BF16),
-        ),
-        in_specs=[
-            pl.BlockSpec(memory_space=pltpu.SMEM if n == 2 else pltpu.VMEM) for n in range(4)
-        ],
-        out_specs=[pl.BlockSpec(memory_space=pltpu.VMEM)] * 3,
-        name="lists",
-    )(
-        block_cols.reshape(1, K),
-        block_rows.reshape(1, K),
-        live_count.reshape(1, 1),
-        owner_order.reshape(1, BLK),
-    )
     return pl.pallas_call(
         kernel,
         out_shape=jax.ShapeDtypeStruct((EP, BLK), F32),
-        in_specs=[anyspace] * 6,
+        in_specs=[anyspace] * 7,
         out_specs=pl.BlockSpec(memory_space=pltpu.VMEM),
         scratch_shapes=[
             vm((EP, SX, SY, NZ), F32), vm((K, BLK, BLK), BF16), vm((3 * NZ, NZ), BF16),
+            vm((1, K), I32), vm((1, K), I32), vm((1, BLK), I32), pltpu.SMEM((1, 1), I32),
             vm((EP, SY, NZ), F32), vm((SX * 4, NZ), F32), vm((8, NZ), F32),
             vm((EP, SY, NZ), F32), vm((SX * 4, NZ), F32), vm((8, NZ), F32),
             vm((2, SX, SY * 4 + 8, BLK), F32), vm((CB * 4, BLK), F32),
             vm((CAP // 8, 32, BLK), F32), vm((NSLAB, MSG, BLK), BF16), vm((NSLAB, MSG, BLK), BF16),
             vm((NSLAB * MSG, BLK), F32), vm((MSG // 2, BLK), F32), vm((K * 4, BLK), F32), vm((BLK, K), BF16),
-            vm((NSLAB, 1, BLK), I32), pltpu.SMEM((NSLAB, 1, BLK), I32),
-            pltpu.SMEM((2, K), I32),
+            vm((NSLAB, 1, BLK), I32), vm((NSLAB, 1, BLK), I32), pltpu.SMEM((NSLAB, 1, BLK), I32),
+            vm((2, K), I32), pltpu.SMEM((2, K), I32),
             vm((BLK * 4, BLK), F32), vm((NSLAB, 32, BLK), F32),
             vm((NSTA, 4, BLK), F32), vm((NSTA, 4, BLK), F32),
             dma((9,)), dma((3,)), dma((3,)), dma((NSLAB,)), dma((NSLAB,)), dma((NSLAB,)), dma((NSLAB,)),
@@ -403,9 +389,10 @@
     )(
         model_change,
         sens_blocks.reshape(K, BLK, BLK),
-        req,
-        lists,
-        routes,
+        block_cols.reshape(1, K),
+        block_rows.reshape(1, K),
+        live_count.reshape(1, 1),
+        owner_order.reshape(1, BLK),
         jnp.asarray(z_matrix()),
     )
 

time: 59.1 us -> 57.6 us (0.975)
  Pallas kernels: 54.3 us -> 51.7 us
  local copies, waits for them, and re-layouts: 3.88 us -> 5 us
    pallas_call x1 -> x0, Pallas kernels: 2.32 us -> none  [on_device(): pl.pallas_call(list_kernel, out_shape=(jax.ShapeDtypeStruct((NSLAB, 1, BL...]
    unnamed x9 -> x11, local copies, waits for them, and re-layouts: 3.88 us -> 5 us
where the time goes in v2:
time: 57.6 us; the launch traced here: 57.4 us
  Pallas kernels  51.7 us (90%)
  local copies, waits for them, and re-layouts  5 us (9%)
  between operations  0.67 us (1%)
    pallas_call x1, Pallas kernels, on_device(): pl.pallas_call(kernel, out_shape=jax.ShapeDtypeStruct((EP, BLK), F32), in...  51.7 us
    unnamed x11, local copies, waits for them, and re-layouts  5 us

profile of v2, /device:TPU:1, one launch (start us, length us, event | category | flops | bytes accessed | tf_op | source)
XLA Modules:
  0.0 57.4 jit_solution(5440879822138400247)
XLA Ops:
  0.7 0.0 copy-start
  0.7 1.4 %copy-done = f32[4,12,32,256]{3,2,1,0:T(8,128)S(1)} copy-done((f32[4,12,32,256]{3,2,1,0:T(8,128)S(1)}, f32[4,12,32,256]{3,2,1,0:T(8,128)}, u32[]{:S(2)}) %copy-start) | copy-done | bytes 1572888
  2.1 0.0 copy-start.1
  2.1 1.0 %copy-done.1 = bf16[768,256]{1,0:T(8,128)(2,1)S(1)} copy-done((bf16[768,256]{1,0:T(8,128)(2,1)S(1)}, bf16[768,256]{1,0:T(8,128)(2,1)}, u32[]{:S(2)}) %copy-start.1) | copy-done | bytes 393240
  3.1 0.0 copy-start.2
  3.1 0.7 %copy-done.2 = s32[1,1,640]{2,1,0:T(1,128)S(1)} copy-done((s32[1,1,640]{2,1,0:T(1,128)S(1)}, s32[1,1,640]{2,1,0:T(1,128)}, u32[]{:S(2)}) %copy-start.2) | copy-done | bytes 2584
  3.7 0.0 copy-start.3
  3.7 0.7 %copy-done.3 = s32[1,1,640]{2,1,0:T(1,128)S(1)} copy-done((s32[1,1,640]{2,1,0:T(1,128)S(1)}, s32[1,1,640]{2,1,0:T(1,128)}, u32[]{:S(2)}) %copy-start.3) | copy-done | bytes 2584
  4.4 0.0 copy-start.4
  4.4 0.7 %copy-done.4 = s32[128]{0:T(128)S(1)} copy-done((s32[128]{0:T(128)S(1)}, s32[128]{0:T(128)}, u32[]{:S(2)}) %copy-start.4) | copy-done | bytes 536
  5.1 51.7 %gravity_step.1 = f32[4,128]{1,0:T(4,128)S(1)} custom-call(f32[4,12,32,256]{3,2,1,0:T(8,128)S(1)} %copy-done, bf16[640,128,128]{2,1,0:T(8,128)(2,1)} %bitcast.7, s32[1,640]{1,0:T(1,128)S(1)} %bitcast.4, s32[1,640]{1,0:T(1,128)S(1)} %bitcast.5, s32[1,1]{1,0:T(1,128)S(6)} %copy.9.live, s32[1,128]{1,0:T(1,128)S(1)} %bitcast.6, bf16[768,256]{1,0:T(8,128)(2,1)S(1)} %copy-done.1), custom_call_target="tpu_custom_call" | custom-call | tf_op jit(solution)/shard_map/gravity_step/pallas_call | solution.py:365
  56.8 0.6 %copy.10 = f32[4,128]{1,0:T(4,128)} copy(f32[4,128]{1,0:T(4,128)S(1)} %gravity_step.1) | data formatting | bytes 4096
Async XLA Ops:
  0.7 1.4 %copy-start = (f32[4,12,32,256]{3,2,1,0:T(8,128)S(1)}, f32[4,12,32,256]{3,2,1,0:T(8,128)}, u32[]{:S(2)}) copy-start(f32[4,12,32,256]{3,2,1,0:T(8,128)} %model.1) | copy-start | bytes 4718596
  2.1 1.0 %copy-start.1 = (bf16[768,256]{1,0:T(8,128)(2,1)S(1)}, bf16[768,256]{1,0:T(8,128)(2,1)}, u32[]{:S(2)}) copy-start(bf16[768,256]{1,0:T(8,128)(2,1)} %constant.2.clone.wz) | copy-start | bytes 1179652
  3.1 0.7 %copy-start.2 = (s32[1,1,640]{2,1,0:T(1,128)S(1)}, s32[1,1,640]{2,1,0:T(1,128)}, u32[]{:S(2)}) copy-start(s32[1,1,640]{2,1,0:T(1,128)} %param.10) | copy-start | bytes 7684
  3.7 0.7 %copy-start.3 = (s32[1,1,640]{2,1,0:T(1,128)S(1)}, s32[1,1,640]{2,1,0:T(1,128)}, u32[]{:S(2)}) copy-start(s32[1,1,640]{2,1,0:T(1,128)} %param.9) | copy-start | bytes 7684
  4.4 0.7 %copy-start.4 = (s32[128]{0:T(128)S(1)}, s32[128]{0:T(128)}, u32[]{:S(2)}) copy-start(s32[128]{0:T(128)} %param.12) | copy-start | bytes 1540

commit v3 on v2

--- a/solution.py
+++ b/solution.py
@@ -27,6 +27,9 @@
 NSLAB, NSTA = 16, 8
 MSG = CAP * EP
 KT = K // BLK
+NDEV = NSLAB * NSTA
+SLICES = ((0, 24), (24, 48), (48, 64), (64, 80))
+GROUP = 32
 
 
 def torus(step):
@@ -52,8 +55,8 @@
 def kernel(
     model, sens, cols, rows, live, owner, wz, out,
     X, sv, wv, cv, rv, ov, lv, Sx, Sy, Sc, Rx, Ry, Rc, D, C, st, send, recv, work, gat, T, R,
-    reqv, reqin, reqs, lists, lists_s, red, redin, acc, accin,
-    lsem, hss, hrs, qss, qrs, ass_, ars, rss, rrs, tss, trs,
+    reqv, reqin, reqs, lists, lists_s, red, outs, ins,
+    lsem, hss, hrs, qss, qrs, ass_, ars, rss, rrs,
 ):
     i, j = lax.axis_index("slab"), lax.axis_index("sta")
     xx, zz = i // 4, lax.rem(i, 4)
@@ -109,10 +112,14 @@
         ties.append(tie_f)
         rels.append(jnp.where(tie, rel, 0))
     count = jnp.broadcast_to(carry, (16, BLK))
-    scan = count
-    for s in (1, 2, 4, 8):
-        scan = scan + jnp.where(sub16 >= s, pltpu.roll(scan, s, 0), 0.0)
-    base = scan - count
+    bases = []
+    for lo, hi in SLICES:
+        inside = jnp.clip(count - lo, 0.0, hi - lo)
+        scan = inside
+        for s in (1, 2, 4, 8):
+            scan = scan + jnp.where(sub16 >= s, pltpu.roll(scan, s, 0), 0.0)
+        before = jnp.sum(jnp.minimum(count, lo), axis=0, keepdims=True)
+        bases.append(before + scan - inside - lo)
 
     place = one(sub128 == ov[...])
     inverse = lax.dot_general(
@@ -124,6 +131,9 @@
     for t in range(KT):
         rank_k = jnp.sum(ties[t] * ranks[t], axis=0, keepdims=True).astype(I32)
         slot_k = jnp.sum(ties[t] * (jnp.minimum(ranks[t], CAP - 1.0) + sub16.astype(F32) * CAP), axis=0, keepdims=True).astype(I32)
+        base = bases[0]
+        for (lo, _), later in zip(SLICES[1:], bases[1:]):
+            base = jnp.where(ranks[t] >= lo, later, base)
         spots.append(jnp.sum(ties[t] * (ranks[t] + base), axis=0, keepdims=True).astype(I32))
         rel = rels[t]
         cell = (rel & -64) + ((rel & 1) << 5) + ((rel >> 1) & 31)
@@ -207,47 +217,38 @@
     to_s = pltpu.make_async_copy(lists, lists_s, lsem.at[7])
     to_s.start()
 
-    halos[0].wait_recv()
-    halos[1].wait_recv()
-    for k in range(SX // 2):
-        s = H0 * Ry[8 * k : 8 * k + 4, :] + H1 * Ry[8 * k + 4 : 8 * k + 8, :]
-        if k < SX // 2 - 1:
-            t = H2 * Ry[8 * k + 8 : 8 * k + 12, :] + H3 * Ry[8 * k + 12 : 8 * k + 16, :]
-        else:
-            t = Rc[0:4, :]
-        lo, hi = s + t, C1 * s + C2 * t
-        for z in range(2):
-            at = slice(z * BLK, (z + 1) * BLK)
-            D[z, 2 * k, SY * 4 : SY * 4 + 4, :] = lo[:, at]
-            D[z, 2 * k + 1, SY * 4 : SY * 4 + 4, :] = hi[:, at]
-
     low = lax.broadcasted_iota(I32, (8, BLK), 0) < 4
     ca, cb = jnp.where(low, H0, -H2), jnp.where(low, H1, H3)
     cc, cd = jnp.where(low, H2, -H0), jnp.where(low, H3, H1)
-    ce = jnp.where(low, 1.0, C2)
+    ce = jnp.where(lax.broadcasted_iota(I32, (8, NZ), 0) < 4, 1.0, C2)
     loads[5].wait()
 
-    def yz(x, _):
+    def y_inner(x):
         parts = []
         for z in range(2):
-            v = D[z, x, 0 : SY * 4, :].reshape(SY // 2, 8, BLK)
+            v = D[z, x].reshape(SY // 2, 8, BLK)
             u = pltpu.roll(v, 4, 1)
-            s = ca * v + cb * u
             t = cc * v[1:] + cd * u[1:]
-            rim = D[z, x, SY * 4 : SY * 4 + 4, :]
-            last = ce * jnp.concatenate([rim, rim], 0)
-            parts.append((s + jnp.concatenate([t, last[None]], 0)).reshape(SY * 4, BLK))
-        full = jnp.concatenate(parts, 1)
+            none = jnp.zeros((1, 8, BLK), F32)
+            parts.append((ca * v + cb * u + jnp.concatenate([t, none], 0)).reshape(SY * 4, BLK))
+        return jnp.concatenate(parts, 1)
+
+    def z_pass(full):
         high = full.astype(BF16)
         rest = (full - high.astype(F32)).astype(BF16)
-        res = jnp.dot(jnp.concatenate([high, rest, high], 1), wv[...], preferred_element_type=F32)
+        return jnp.dot(jnp.concatenate([high, rest, high], 1), wv[...], preferred_element_type=F32)
+
+    def yz(x, _):
+        res = z_pass(y_inner(x))
         at = pl.multiple_of(x * 2 * SY * 4, 2 * SY * 4)
         C[pl.ds(at, SY * 4), :] = res[:, :BLK]
         C[pl.ds(at + SY * 4, SY * 4), :] = res[:, BLK:]
         return 0
 
     lax.fori_loop(0, SX - 2, yz, 0)
-    halos[2].wait_recv()
+
+    for cp in halos:
+        cp.wait_recv()
     for e in range(EP):
         for q in range(SY // 8):
             at = slice(8 * q, 8 * q + 8)
@@ -256,6 +257,20 @@
             spread(SX - 2, e, q, s + t)
             spread(SX - 1, e, q, C1 * s + C2 * t)
     lax.fori_loop(SX - 2, SX, yz, 0)
+    rims = []
+    for k in range(SX // 2):
+        s = H0 * Ry[8 * k : 8 * k + 4, :] + H1 * Ry[8 * k + 4 : 8 * k + 8, :]
+        if k < SX // 2 - 1:
+            t = H2 * Ry[8 * k + 8 : 8 * k + 12, :] + H3 * Ry[8 * k + 12 : 8 * k + 16, :]
+        else:
+            t = Rc[0:4, :]
+        for rim in (s + t, C1 * s + C2 * t):
+            rims.append(ce * jnp.concatenate([rim, rim], 0))
+    added = z_pass(jnp.concatenate(rims, 0))
+    for x in range(SX):
+        for z in range(2):
+            at = (2 * x + z + 1) * SY * 4 - 8
+            C[at : at + 8, :] = C[at : at + 8, :] + added[8 * x : 8 * x + 8, z * BLK : (z + 1) * BLK]
 
     for cp in asks:
         cp.wait_recv()
@@ -264,41 +279,41 @@
     to_r.wait()
     to_s.wait()
 
-    def pack(n):
+    def pack(n, lo, hi):
         def some(g, _):
             for a in range(8):
                 c = reqs[n, 0, g * 8 + a]
                 st[g, 4 * a : 4 * a + 4, :] = C[pl.ds(c * 4, 4), :]
             return 0
 
-        lax.fori_loop(0, CAP // 8, some, 0)
-
-    msgs = []
-    for n in list(range(1, NSLAB)) + [0]:
-        pack(n)
-        if n == 0:
-            work[0:MSG, :] = st[...].reshape(MSG, BLK).astype(BF16).astype(F32)
-            break
-        send[n] = st[...].reshape(MSG, BLK).astype(BF16)
-        cp = pltpu.make_async_remote_copy(
-            send.at[n], recv.at[n], ass_.at[n], ars.at[n], device_id=(ahead(n), j), device_id_type=MESH
-        )
-        cp.start()
-        msgs.append(cp)
+        lax.fori_loop(lo // 8, hi // 8, some, 0)
+        return st[lo // 8 : hi // 8].reshape((hi - lo) * 4, BLK).astype(BF16)
+
+    msgs = {}
+    for m, (lo, hi) in enumerate(SLICES):
+        at = pl.ds(4 * lo, 4 * (hi - lo))
+        for n in range(1, NSLAB):
+            send[n, at, :] = pack(n, lo, hi)
+            sem = m * NSLAB + n
+            msgs[m, n] = pltpu.make_async_remote_copy(
+                send.at[n, at, :], recv.at[n, at, :], ass_.at[sem], ars.at[sem],
+                device_id=(ahead(n), j), device_id_type=MESH,
+            )
+            msgs[m, n].start()
+    work[0:MSG, :] = pack(0, 0, CAP).astype(F32)
 
     loads[6].wait()
     first_half = lax.broadcasted_iota(I32, (8, BLK), 0) < 4
-    HALF = CAP // 2
 
     def products(g, _):
-        for a in range(HALF):
-            c = lists_s[1, g * HALF + a]
+        for a in range(GROUP):
+            c = lists_s[1, g * GROUP + a]
             gat[4 * a : 4 * a + 4, :] = work[pl.ds(c * 4, 4), :]
-        for a in range(0, HALF, 2):
+        for a in range(0, GROUP, 2):
             lhs = gat[4 * a : 4 * a + 8, :].astype(BF16)
-            rhs = jnp.concatenate([sv[lists_s[0, g * HALF + a]], sv[lists_s[0, g * HALF + a + 1]]], 0)
+            rhs = jnp.concatenate([sv[lists_s[0, g * GROUP + a]], sv[lists_s[0, g * GROUP + a + 1]]], 0)
             res = lax.dot_general(lhs, rhs, NT, preferred_element_type=F32)
-            at = pl.multiple_of(g * HALF * 4, HALF * 4) + 4 * a
+            at = pl.multiple_of(g * GROUP * 4, GROUP * 4) + 4 * a
             T[pl.ds(at, 8), :] = jnp.where(first_half, res[:, :BLK], res[:, BLK:])
         return 0
 
@@ -314,47 +329,39 @@
             )
         return sums
 
-    for n in range(1, NSLAB):
-        msgs[n - 1].wait_recv()
-        work[n * MSG : (n + 1) * MSG, :] = recv[n].astype(F32)
-        if n >= NSLAB // 2:
-            c = n - NSLAB // 2
-            lax.fori_loop(2 * c, 2 * c + 2, products, 0)
-        if n == NSLAB - 2:
+    for m, (lo, hi) in enumerate(SLICES):
+        for n in range(1, NSLAB):
+            msgs[m, n].wait_recv()
+            work[n * MSG + 4 * lo : n * MSG + 4 * hi, :] = recv[n, 4 * lo : 4 * hi, :].astype(F32)
+        lax.fori_loop(8 * lo // GROUP, 8 * hi // GROUP, products, 0)
+        if hi == 64:
             for e, part in enumerate(route(0, 512)):
                 red[pl.ds(e, BLK, stride=4), :] = part
     for e, part in enumerate(route(512, K)):
         red[pl.ds(e, BLK, stride=4), :] = red[pl.ds(e, BLK, stride=4), :] + part
-
-    sums = []
-    for n in range(1, NSLAB):
-        p = ahead(n)
-        cp = pltpu.make_async_remote_copy(
-            red.at[pl.ds(pl.multiple_of(p * 32, 32), 32), :], redin.at[n],
-            rss.at[n], rrs.at[n], device_id=(p, j), device_id_type=MESH,
-        )
-        cp.start()
-        sums.append(cp)
-    total = red[pl.ds(pl.multiple_of(i * 32, 32), 32), :]
-    for n in range(1, NSLAB):
-        sums[n - 1].wait_recv()
-        total = total + redin[n]
-    for q in range(NSTA):
-        acc[q] = total[4 * q : 4 * q + 4]
-    lasts = []
-    for t in range(1, NSTA):
-        q = lax.rem(j + t, NSTA)
-        cp = pltpu.make_async_remote_copy(
-            acc.at[q], accin.at[t], tss.at[t], trs.at[t], device_id=(i, q), device_id_type=MESH
-        )
-        cp.start()
-        lasts.append(cp)
-    final = acc[j]
-    for t in range(1, NSTA):
-        lasts[t - 1].wait_recv()
-        final = final + accin[t]
-    out[...] = final
-    for cp in halos + asks + msgs + sums + lasts:
+    for b in range(NDEV):
+        outs[b] = red[4 * b : 4 * b + 4, :]
+
+    me = i * NSTA + j
+
+    def give(t, _):
+        d = lax.rem(me + t, NDEV)
+        pltpu.make_async_remote_copy(
+            outs.at[d], ins.at[me], rss.at[0], rrs.at[0],
+            device_id=(d // NSTA, lax.rem(d, NSTA)), device_id_type=MESH,
+        ).start()
+        return 0
+
+    lax.fori_loop(1, NDEV, give, 0)
+    ins[me] = outs[me]
+    rest = pl.ds(0, NDEV - 1)
+    every = pltpu.make_async_remote_copy(
+        outs.at[rest], ins.at[rest], rss.at[0], rrs.at[0], device_id=(i, j), device_id_type=MESH
+    )
+    every.wait_recv()
+    out[...] = jnp.sum(jnp.sum(ins[...].reshape(8, NDEV // 8, 4, BLK), axis=1), axis=0)
+    every.wait_send()
+    for cp in halos + asks + list(msgs.values()):
         cp.wait_send()
 
 
@@ -372,18 +379,17 @@
             vm((1, K), I32), vm((1, K), I32), vm((1, BLK), I32), pltpu.SMEM((1, 1), I32),
             vm((EP, SY, NZ), F32), vm((SX * 4, NZ), F32), vm((8, NZ), F32),
             vm((EP, SY, NZ), F32), vm((SX * 4, NZ), F32), vm((8, NZ), F32),
-            vm((2, SX, SY * 4 + 8, BLK), F32), vm((CB * 4, BLK), F32),
+            vm((2, SX, SY * 4, BLK), F32), vm((CB * 4, BLK), F32),
             vm((CAP // 8, 32, BLK), F32), vm((NSLAB, MSG, BLK), BF16), vm((NSLAB, MSG, BLK), BF16),
-            vm((NSLAB * MSG, BLK), F32), vm((MSG // 2, BLK), F32), vm((K * 4, BLK), F32), vm((BLK, K), BF16),
+            vm((NSLAB * MSG, BLK), F32), vm((GROUP * 4, BLK), F32), vm((K * 4, BLK), F32), vm((BLK, K), BF16),
             vm((NSLAB, 1, BLK), I32), vm((NSLAB, 1, BLK), I32), pltpu.SMEM((NSLAB, 1, BLK), I32),
             vm((2, K), I32), pltpu.SMEM((2, K), I32),
-            vm((BLK * 4, BLK), F32), vm((NSLAB, 32, BLK), F32),
-            vm((NSTA, 4, BLK), F32), vm((NSTA, 4, BLK), F32),
-            dma((9,)), dma((3,)), dma((3,)), dma((NSLAB,)), dma((NSLAB,)), dma((NSLAB,)), dma((NSLAB,)),
-            dma((NSLAB,)), dma((NSLAB,)), dma((NSTA,)), dma((NSTA,)),
+            vm((BLK * 4, BLK), F32), vm((NDEV, 4, BLK), F32), vm((NDEV, 4, BLK), F32),
+            dma((9,)), dma((3,)), dma((3,)), dma((NSLAB,)), dma((NSLAB,)),
+            dma((4 * NSLAB,)), dma((4 * NSLAB,)), dma((1,)), dma((1,)),
         ],
         compiler_params=pltpu.CompilerParams(
-            collective_id=0, has_side_effects=True, vmem_limit_bytes=52 * 2**20
+            collective_id=0, has_side_effects=True, vmem_limit_bytes=60 * 2**20
         ),
         name="gravity_step",
     )(

time: 57.6 us -> 47.2 us (0.82)
  Pallas kernels: 51.7 us -> 45.1 us
  local copies, waits for them, and re-layouts: 5 us -> 1.26 us
    pallas_call x1, Pallas kernels: 51.7 us -> 45.1 us  [on_device(): pl.pallas_call(kernel, out_shape=jax.ShapeDtypeStruct((EP, BLK), F32), in...]
    unnamed x11 -> x1, local copies, waits for them, and re-layouts: 5 us -> 1.26 us
where the time goes in v3:
time: 47.2 us; the launch traced here: 47 us
  Pallas kernels  45.1 us (96%)
  local copies, waits for them, and re-layouts  1.26 us (3%)
  between operations  0.66 us (1%)
    pallas_call x1, Pallas kernels, on_device(): pl.pallas_call(kernel, out_shape=jax.ShapeDtypeStruct((EP, BLK), F32), in...  45.1 us
    unnamed x1, local copies, waits for them, and re-layouts  1.26 us

profile of v3, /device:TPU:1, one launch (start us, length us, event | category | flops | bytes accessed | tf_op | source)
XLA Modules:
  0.0 47.0 jit_solution(13365026175538084191)
XLA Ops:
  0.7 45.1 %gravity_step.1 = f32[4,128]{1,0:T(4,128)} custom-call(f32[4,12,32,256]{3,2,1,0:T(8,128)} %model.1, bf16[640,128,128]{2,1,0:T(8,128)(2,1)} %bitcast.4, s32[1,640]{1,0:T(1,128)} %bitcast.5, s32[1,640]{1,0:T(1,128)} %bitcast.6, s32[1,1]{1,0:T(1,128)S(6)} %copy.9.live, s32[1,128]{1,0:T(1,128)} %bitcast.7, bf16[768,256]{1,0:T(8,128)(2,1)} %constant.2.clone.wz), custom_call_target="tpu_custom_call" | custom-call | tf_op jit(solution)/shard_map/gravity_step/pallas_call | solution.py:372
  45.8 1.3 %copy.10 = f32[4,128]{1,0:T(4,128)} copy(f32[4,128]{1,0:T(4,128)} %gravity_step.1) | data formatting | bytes 4096

commit v4 on v3

--- a/solution.py
+++ b/solution.py
@@ -37,7 +37,7 @@
     return min(dx, 4 - dx) + min(dz, 4 - dz)
 
 
-STEPS = [(0, 0)] + [divmod(s, 4) for s in sorted(range(1, 16), key=lambda s: -torus(s))]
+STEPS = [(0, 0), (2, 2), (1, 2), (3, 2), (2, 1), (2, 3), (1, 1), (3, 3), (1, 3), (3, 1), (2, 0), (0, 2), (1, 0), (0, 1), (3, 0), (0, 3)]
 
 
 def z_matrix():
@@ -70,13 +70,17 @@
     for cp in loads:
         cp.start()
 
-    def ahead(n):
-        dx, dz = STEPS[n]
-        return lax.rem(xx + dx, 4) * 4 + lax.rem(zz + dz, 4)
-
-    def behind(n):
-        dx, dz = STEPS[n]
-        return lax.rem(xx + 4 - dx, 4) * 4 + lax.rem(zz + 4 - dz, 4)
+    core = lax.rem(j, 2)
+
+    def partner(n, sign):
+        dx, dz = ((sign * d) % 4 for d in STEPS[n])
+        mx, mz = (1 * dz) % 4, (1 * dx) % 4
+        ax = dx + core * (mx - dx)
+        az = dz + core * (mz - dz)
+        return lax.rem(xx + ax, 4) * 4 + lax.rem(zz + az, 4)
+
+    ahead = functools.partial(partner, sign=1)
+    behind = functools.partial(partner, sign=-1)
 
     up_i, down_i = lax.rem(i + 1, NSLAB), lax.rem(i + NSLAB - 1, NSLAB)
     up_j, down_j = lax.rem(j + 1, NSTA), lax.rem(j + NSTA - 1, NSTA)
@@ -352,7 +356,13 @@
         ).start()
         return 0
 
-    lax.fori_loop(1, NDEV, give, 0)
+    def gives(g, _):
+        for a in range(7):
+            give(1 + g * 7 + a, 0)
+        return 0
+
+    lax.fori_loop(0, 18, gives, 0)
+    give(127, 0)
     ins[me] = outs[me]
     rest = pl.ds(0, NDEV - 1)
     every = pltpu.make_async_remote_copy(
@@ -368,6 +378,7 @@
 def on_device(model_change, sens_blocks, block_rows, block_cols, live_count, owner_order):
     anyspace = pl.BlockSpec(memory_space=pl.ANY)
     dma = pltpu.SemaphoreType.DMA
+    keep = functools.partial(pltpu.with_memory_space_constraint, memory_space=pltpu.HBM)
     vm = pltpu.VMEM
     return pl.pallas_call(
         kernel,
@@ -386,20 +397,20 @@
             vm((2, K), I32), pltpu.SMEM((2, K), I32),
             vm((BLK * 4, BLK), F32), vm((NDEV, 4, BLK), F32), vm((NDEV, 4, BLK), F32),
             dma((9,)), dma((3,)), dma((3,)), dma((NSLAB,)), dma((NSLAB,)),
-            dma((4 * NSLAB,)), dma((4 * NSLAB,)), dma((1,)), dma((1,)),
+            dma((len(SLICES) * NSLAB,)), dma((len(SLICES) * NSLAB,)), dma((1,)), dma((1,)),
         ],
         compiler_params=pltpu.CompilerParams(
-            collective_id=0, has_side_effects=True, vmem_limit_bytes=60 * 2**20
+            collective_id=0, has_side_effects=True, vmem_limit_bytes=52 * 2**20
         ),
         name="gravity_step",
     )(
-        model_change,
-        sens_blocks.reshape(K, BLK, BLK),
-        block_cols.reshape(1, K),
-        block_rows.reshape(1, K),
+        keep(model_change),
+        keep(sens_blocks.reshape(K, BLK, BLK)),
+        keep(block_cols.reshape(1, K)),
+        keep(block_rows.reshape(1, K)),
         live_count.reshape(1, 1),
-        owner_order.reshape(1, BLK),
-        jnp.asarray(z_matrix()),
+        keep(owner_order.reshape(1, BLK)),
+        keep(jnp.asarray(z_matrix())),
     )
 
 

time: 47.2 us -> 45.7 us (0.968)
  Pallas kernels: 45.1 us -> 44.3 us
  local copies, waits for them, and re-layouts: 1.26 us -> 0.58 us
    pallas_call x1, Pallas kernels: 45.1 us -> 44.3 us  [on_device(): pl.pallas_call(kernel, out_shape=jax.ShapeDtypeStruct((EP, BLK), F32), in...]
    unnamed x1, local copies, waits for them, and re-layouts: 1.26 us -> 0.58 us
where the time goes in v4:
time: 45.7 us; the launch traced here: 45.6 us
  Pallas kernels  44.3 us (97%)
  between operations  0.66 us (1%)
  local copies, waits for them, and re-layouts  0.58 us (1%)
    pallas_call x1, Pallas kernels, on_device(): pl.pallas_call(kernel, out_shape=jax.ShapeDtypeStruct((EP, BLK), F32), in...  44.3 us

profile of v4, /device:TPU:1, one launch (start us, length us, event | category | flops | bytes accessed | tf_op | source)
XLA Modules:
  0.0 45.6 jit_solution(1635232567446030430)
XLA Ops:
  0.7 44.3 %gravity_step.1 = f32[4,128]{1,0:T(4,128)S(1)} custom-call(f32[4,12,32,256]{3,2,1,0:T(8,128)} %model.1, bf16[640,128,128]{2,1,0:T(8,128)(2,1)} %bitcast.4, s32[1,640]{1,0:T(1,128)} %bitcast.5, s32[1,640]{1,0:T(1,128)} %bitcast.6, s32[1,1]{1,0:T(1,128)S(6)} %copy.9.live, s32[1,128]{1,0:T(1,128)} %bitcast.7, bf16[768,256]{1,0:T(8,128)(2,1)} %constant.2.clone.wz), custom_call_target="tpu_custom_call" | custom-call | tf_op jit(solution)/shard_map/gravity_step/pallas_call | solution.py:383
  45.0 0.6 %copy.10 = f32[4,128]{1,0:T(4,128)} copy(f32[4,128]{1,0:T(4,128)S(1)} %gravity_step.1) | data formatting | bytes 4096

commit v5 on v4

--- a/solution.py
+++ b/solution.py
@@ -29,7 +29,7 @@
 KT = K // BLK
 NDEV = NSLAB * NSTA
 SLICES = ((0, 24), (24, 48), (48, 64), (64, 80))
-GROUP = 32
+GROUP = 64
 
 
 def torus(step):

time: 45.7 us -> 44.7 us (0.978)
  Pallas kernels: 44.3 us -> 43.3 us
    pallas_call x1, Pallas kernels: 44.3 us -> 43.3 us  [on_device(): pl.pallas_call(kernel, out_shape=jax.ShapeDtypeStruct((EP, BLK), F32), in...]
where the time goes in v5:
time: 44.7 us; the launch traced here: 44.6 us
  Pallas kernels  43.3 us (97%)
  between operations  0.66 us (1%)
  local copies, waits for them, and re-layouts  0.58 us (1%)
    pallas_call x1, Pallas kernels, on_device(): pl.pallas_call(kernel, out_shape=jax.ShapeDtypeStruct((EP, BLK), F32), in...  43.3 us

profile of v5, /device:TPU:1, one launch (start us, length us, event | category | flops | bytes accessed | tf_op | source)
XLA Modules:
  0.0 44.6 jit_solution(13405487452031725318)
XLA Ops:
  0.7 43.3 %gravity_step.1 = f32[4,128]{1,0:T(4,128)S(1)} custom-call(f32[4,12,32,256]{3,2,1,0:T(8,128)} %model.1, bf16[640,128,128]{2,1,0:T(8,128)(2,1)} %bitcast.4, s32[1,640]{1,0:T(1,128)} %bitcast.5, s32[1,640]{1,0:T(1,128)} %bitcast.6, s32[1,1]{1,0:T(1,128)S(6)} %copy.9.live, s32[1,128]{1,0:T(1,128)} %bitcast.7, bf16[768,256]{1,0:T(8,128)(2,1)} %constant.2.clone.wz), custom_call_target="tpu_custom_call" | custom-call | tf_op jit(solution)/shard_map/gravity_step/pallas_call | solution.py:383
  44.0 0.6 %copy.10 = f32[4,128]{1,0:T(4,128)} copy(f32[4,128]{1,0:T(4,128)S(1)} %gravity_step.1) | data formatting | bytes 4096

commit v6 on v5

--- a/solution.py
+++ b/solution.py
@@ -368,11 +368,11 @@
     every = pltpu.make_async_remote_copy(
         outs.at[rest], ins.at[rest], rss.at[0], rrs.at[0], device_id=(i, j), device_id_type=MESH
     )
+    for cp in halos + asks + list(msgs.values()):
+        cp.wait_send()
     every.wait_recv()
     out[...] = jnp.sum(jnp.sum(ins[...].reshape(8, NDEV // 8, 4, BLK), axis=1), axis=0)
     every.wait_send()
-    for cp in halos + asks + list(msgs.values()):
-        cp.wait_send()
 
 
 def on_device(model_change, sens_blocks, block_rows, block_cols, live_count, owner_order):

time: 44.7 us -> 44.6 us (level)
  no operation moved by 1% of the time
where the time goes in v6:
time: 44.6 us; the launch traced here: 44.5 us
  Pallas kernels  43.2 us (97%)
  between operations  0.66 us (1%)
  local copies, waits for them, and re-layouts  0.58 us (1%)
    pallas_call x1, Pallas kernels, on_device(): pl.pallas_call(kernel, out_shape=jax.ShapeDtypeStruct((EP, BLK), F32), in...  43.2 us

profile of v6, /device:TPU:1, one launch (start us, length us, event | category | flops | bytes accessed | tf_op | source)
XLA Modules:
  0.0 44.5 jit_solution(2438486056893084636)
XLA Ops:
  0.7 43.2 %gravity_step.1 = f32[4,128]{1,0:T(4,128)S(1)} custom-call(f32[4,12,32,256]{3,2,1,0:T(8,128)} %model.1, bf16[640,128,128]{2,1,0:T(8,128)(2,1)} %bitcast.4, s32[1,640]{1,0:T(1,128)} %bitcast.5, s32[1,640]{1,0:T(1,128)} %bitcast.6, s32[1,1]{1,0:T(1,128)S(6)} %copy.9.live, s32[1,128]{1,0:T(1,128)} %bitcast.7, bf16[768,256]{1,0:T(8,128)(2,1)} %constant.2.clone.wz), custom_call_target="tpu_custom_call" | custom-call | tf_op jit(solution)/shard_map/gravity_step/pallas_call | solution.py:383
  43.9 0.6 %copy.10 = f32[4,128]{1,0:T(4,128)} copy(f32[4,128]{1,0:T(4,128)S(1)} %gravity_step.1) | data formatting | bytes 4096
